TPU v7x, 256 devices: a whole 4x4x8 slice. The times are simulated.
256 devices in a mesh: seq: 64 (over z, x, core), grp: 4 (over y).
Axes of the slice: x: 4, y: 4, z: 8, core: 2. Of those that a mesh axis runs over, the one named last changes fastest.
Arguments:
- patches: bfloat16 [262144, 1024], P(('seq', 'grp')), may hold values from -6 to 6
- dest_map: int32 [256, 64], P(('seq', 'grp')), may hold values from 0 to 63, each once within a row
- series_ids: int32 [64, 64], P('seq'), may hold values from 0 to 15, never falling along the last dimension, each value on 1 to 32 neighbouring positions
- lengths: int32 [64, 64], P('seq'), may hold values from 1 to 64
- w_qkv: bfloat16 [1024, 3072], replicated
- w_out: bfloat16 [1024, 1024], replicated, may hold values from -0.1875 to 0.1875
- gain_var: float32 [1024], replicated, may hold values from 0.1 to 1.9
- gain_time: float32 [1024], replicated, may hold values from 0.1 to 1.9
Outputs:
- mixed: bfloat16 [262144, 1024], P(('seq', 'grp'))
Inputs may be any that keep to these rules, and one draw needn't show every extreme that they name: Each row of dest_map names every index along seq once. `series_ids`: series numbers never fall along a pack's variate slots.
All inputs are finite; a program needn't handle non-finite values.
Results may differ from a plain program's by a relative error of at most 0.012.
Values may be sent and summed in bfloat16 or wider, within the bound.
A program may use at most 192 MiB of HBM per device.

v0:
```python
import jax
import jax.numpy as jnp
from jax import lax
from jax.sharding import PartitionSpec as P

HEADS = 16
TIME = 64
VAR = 64


def rms_norm(values, gain):
    wide = values.astype(jnp.float32)
    scale = lax.rsqrt(jnp.mean(wide * wide, axis=-1, keepdims=True) + 1e-05)
    return (wide * scale * gain).astype(jnp.bfloat16)


def project(normed, w_qkv):
    first_dim, second_dim, width = normed.shape
    proj = jnp.dot(
        normed.reshape(first_dim * second_dim, width), w_qkv, preferred_element_type=jnp.float32
    ).astype(jnp.bfloat16)
    proj = proj.reshape(first_dim, second_dim, 3, HEADS, width // HEADS)
    return (proj[:, :, 0], proj[:, :, 1], proj[:, :, 2])


def attend(query, keys, values, keep, form_scores, form_context, w_out):
    scores = jnp.einsum(form_scores, query, keys, preferred_element_type=jnp.float32) * query.shape[
        -1
    ] ** (-0.5)
    scores = jnp.where(keep, scores, -1e30)
    scores = scores - jnp.max(scores, axis=-1, keepdims=True)
    expo = jnp.exp(scores)
    weights = (expo / jnp.sum(expo, axis=-1, keepdims=True)).astype(jnp.bfloat16)
    context = jnp.einsum(form_context, weights, values, preferred_element_type=jnp.float32).astype(
        jnp.bfloat16
    )
    first_dim, second_dim = (context.shape[0], context.shape[1])
    flat = context.reshape(first_dim * second_dim, -1)
    return jnp.dot(flat, w_out, preferred_element_type=jnp.float32).reshape(
        first_dim, second_dim, -1
    )


def on_device(patches, dest_map, series_ids, lengths, w_qkv, w_out, gain_var, gain_time):
    rows, width = patches.shape
    n_seq = lax.axis_size("seq")
    n_grp = lax.axis_size("grp")
    block = rows // n_seq
    order = jnp.argsort(dest_map[0])
    outgoing = patches.reshape(n_seq, block, width)[order]
    packed = lax.all_to_all(outgoing, "seq", split_axis=0, concat_axis=0, tiled=True)
    local_times = TIME // n_grp
    packed = packed.reshape(local_times, VAR, width)
    ids = series_ids[0]
    same = (ids[:, None] == ids[None, :])[None, None, :, :]
    query, keys, values = project(rms_norm(packed, gain_var), w_qkv)
    branch = attend(query, keys, values, same, "glhe,gmhe->ghlm", "ghlm,gmhe->glhe", w_out)
    first = (packed.astype(jnp.float32) + branch).astype(jnp.bfloat16)
    share = VAR // n_grp
    spread = first.reshape(local_times, n_grp, share, width)
    turned = lax.all_to_all(spread, "grp", split_axis=1, concat_axis=0, tiled=True).reshape(
        TIME, share, width
    )
    mine = lax.dynamic_slice_in_dim(lengths[0], lax.axis_index("grp") * share, share)
    valid = jnp.arange(TIME)[None, None, None, :] < mine[:, None, None, None]
    query, keys, values = project(rms_norm(turned, gain_time), w_qkv)
    branch = attend(query, keys, values, valid, "lghe,mghe->ghlm", "ghlm,mghe->lghe", w_out)
    second = (turned.astype(jnp.float32) + branch).astype(jnp.bfloat16)
    back = lax.all_to_all(
        second.reshape(n_grp, local_times, share, width),
        "grp",
        split_axis=0,
        concat_axis=2,
        tiled=True,
    )
    return back.reshape(rows, width)


def solution(mesh):
    return jax.shard_map(
        on_device,
        mesh=mesh,
        in_specs=(
            P(("seq", "grp"), None),
            P(("seq", "grp"), None),
            P("seq", None),
            P("seq", None),
            P(),
            P(),
            P(),
            P(),
        ),
        out_specs=P(("seq", "grp"), None),
        check_vma=False,
    )
```

profile of v0, /device:TPU:32, one launch (start us, length us, event | category | flops | bytes accessed | tf_op | source)
XLA Modules:
  0.0 269.2 jit_solution(16259481065179261871)
XLA Ops:
  0.0 0.0 copy-start
  0.0 2.8 %sort.17 = (s32[64]{0:T(128)}, s32[64]{0:T(128)S(1)}) sort(s32[64]{0:T(128)} %bitcast.88, s32[64]{0:T(128)S(1)} %iota.12), dimensions={0}, to_apply=%region_0.0 | sort | flops 384 | bytes 1024 | tf_op jit(solution)/shard_map/jit(argsort)/sort | solution.py:49
  2.9 0.0 copy-done
  2.9 0.0 copy-start.7
  2.9 2.0 gather_fusion
  4.9 11.7 %all-to-all-start = ((bf16[64,16,1024]{2,1,0:T(8,128)(2,1)}), bf16[64,16,1024]{2,1,0:T(8,128)(2,1)S(1)}, u32[]{:S(2)}, u32[]{:S(2)}) async-start(bf16[64,16,1024]{2,1,0:T(8,128)(2,1)} %gather_fusion), calls=%async_computation | async-start | bytes 4194304 | tf_op jit(solution)/shard_map/all_to_all | solution.py:51
  16.6 0.0 copy-done.7
  16.6 0.1 broadcast_compare_fusion
  16.7 50.3 %all-to-all-done = bf16[64,16,1024]{2,1,0:T(8,128)(2,1)S(1)} async-done(((bf16[64,16,1024]{2,1,0:T(8,128)(2,1)}), bf16[64,16,1024]{2,1,0:T(8,128)(2,1)S(1)}, u32[]{:S(2)}, u32[]{:S(2)}) %all-to-all-start) | async-done | bytes 2097184 | tf_op jit(solution)/shard_map/all_to_all | solution.py:51
  67.0 0.5 multiply_reduce_fusion.1
  67.5 0.1 rsqrt.23
  67.6 0.0 copy-done.5
  67.6 0.5 fusion.14
  68.1 11.3 %convolution_convert_fusion.1 = bf16[1024,3072]{1,0:T(8,128)(2,1)} fusion(bf16[1024,1024]{1,0:T(8,128)(2,1)S(1)} %fusion.14, bf16[1024,3072]{1,0:T(8,128)(2,1)} %param.12), kind=kOutput, calls=%fused_computation.12 | convolution fusion | flops 6445596672 | bytes 14680064 | tf_op jit(solution)/shard_map/dot_general | solution.py:19
  79.5 15.9 %reshape.149 = bf16[16,64,3,16,64]{4,3,2,1,0:T(8,128)(2,1)} reshape(bf16[1024,3072]{1,0:T(8,128)(2,1)} %convolution_convert_fusion.1) | data formatting | bytes 12582912 | tf_op jit(solution)/shard_map/reshape | solution.py:22
  95.4 9.2 %fusion.41 = (bf16[16,64,1,16,64]{4,3,2,1,0:T(8,128)(2,1)}, bf16[16,64,1,16,64]{4,3,2,1,0:T(8,128)(2,1)}, bf16[16,64,1,16,64]{4,3,2,1,0:T(8,128)(2,1)}) fusion(bf16[16,64,3,16,64]{4,3,2,1,0:T(8,128)(2,1)} %reshape.149), kind=kLoop, calls=%fused_computation.61 | loop fusion | bytes 12582912 | tf_op jit(solution)/shard_map/slice | solution.py:23
  104.6 7.1 %copy.36 = bf16[16,64,1,16,64]{1,4,3,0,2:T(8,128)(2,1)} copy(bf16[16,64,1,16,64]{4,3,2,1,0:T(8,128)(2,1)} %get-tuple-element.10) | data formatting | bytes 4194304
  111.7 5.8 %fusion.7 = f32[16,16,64,64]{2,3,1,0:T(8,128)S(1)} fusion(bf16[16,64,1,16,64]{4,3,2,1,0:T(8,128)(2,1)} %get-tuple-element.11, bf16[16,64,1,16,64]{4,3,2,1,0:T(8,128)(2,1)} %get-tuple-element.12), kind=kOutput, calls=%fused_computation.19 | convolution fusion | flops 134217728 | bytes 8388608 | tf_op jit(solution)/shard_map/glhe,gmhe->ghlm/dot_general | solution.py:27
  117.5 4.5 %fusion.42 = (f32[16,16,64]{2,1,0:T(8,128)S(1)}, f32[16,16,64,64]{2,3,1,0:T(8,128)}) fusion(f32[16,16,64,64]{2,3,1,0:T(8,128)S(1)} %fusion.7, pred[64,64]{0,1:T(8,128)(4,1)S(1)} %broadcast_compare_fusion), kind=kOutput, calls=%fused_computation.62 | output fusion | flops 6291519 | bytes 8458240 | tf_op jit(solution)/shard_map/sub | solution.py:31
  122.0 0.0 copy-done.2
  122.0 4.9 %fusion.27 = bf16[16,16,64,64]{3,2,1,0:T(8,128)(2,1)S(1)} fusion(f32[16,16,64,64]{2,3,1,0:T(8,128)} %get-tuple-element.14, f32[16,16,64]{2,1,0:T(8,128)S(1)} %get-tuple-element.13, bf16[16,64,1,16,64]{1,4,3,0,2:T(8,128)(2,1)S(1)} %copy-done.2), kind=kOutput, calls=%fused_computation.44 | convolution fusion | flops 137363456 | bytes 8454144 | tf_op jit(solution)/shard_map/ghlm,gmhe->glhe/dot_general | solution.py:34
  127.0 0.0 copy-done.4
  127.0 2.4 fusion.32
  129.4 0.5 convert_element_type.104
  129.9 1.1 fusion.15
  131.0 0.0 copy-start.8
  131.0 1.6 copy.26
  132.7 4.6 %all-to-all-start.1 = ((bf16[16,4,16,1024]{3,2,0,1:T(8,128)(2,1)}), bf16[16,4,16,1024]{3,2,0,1:T(8,128)(2,1)S(1)}, u32[]{:S(2)}, u32[]{:S(2)}) async-start(bf16[16,4,16,1024]{3,2,0,1:T(8,128)(2,1)} %copy.26), calls=%async_computation.1 | async-start | bytes 4194304 | tf_op jit(solution)/shard_map/all_to_all | solution.py:61
  137.3 0.0 copy-done.8
  137.3 0.1 dynamic-slice_bitcast_fusion
  137.3 0.1 iota_compare_fusion
  137.4 26.2 %all-to-all-done.1 = bf16[16,4,16,1024]{3,2,0,1:T(8,128)(2,1)S(1)} async-done(((bf16[16,4,16,1024]{3,2,0,1:T(8,128)(2,1)}), bf16[16,4,16,1024]{3,2,0,1:T(8,128)(2,1)S(1)}, u32[]{:S(2)}, u32[]{:S(2)}) %all-to-all-start.1) | async-done | bytes 2097184 | tf_op jit(solution)/shard_map/all_to_all | solution.py:61
  163.6 0.5 multiply_reduce_fusion
  164.1 0.1 rsqrt.25
  164.2 0.0 copy-done.6
  164.2 0.5 fusion.9
  164.8 11.3 %convolution_convert_fusion = bf16[1024,3072]{1,0:T(8,128)(2,1)} fusion(bf16[1024,1024]{1,0:T(8,128)(2,1)S(1)} %fusion.9, bf16[1024,3072]{1,0:T(8,128)(2,1)} %param.12), kind=kOutput, calls=%fused_computation.11 | convolution fusion | flops 6445596672 | bytes 14680064 | tf_op jit(solution)/shard_map/dot_general | solution.py:19
  176.1 15.9 %reshape.151 = bf16[64,16,3,16,64]{4,3,2,1,0:T(8,128)(2,1)} reshape(bf16[1024,3072]{1,0:T(8,128)(2,1)} %convolution_convert_fusion) | data formatting | bytes 12582912 | tf_op jit(solution)/shard_map/reshape | solution.py:22
  192.0 9.2 %fusion.40 = (bf16[64,16,1,16,64]{4,3,2,1,0:T(8,128)(2,1)}, bf16[64,16,1,16,64]{4,3,2,1,0:T(8,128)(2,1)}, bf16[64,16,1,16,64]{4,3,2,1,0:T(8,128)(2,1)}) fusion(bf16[64,16,3,16,64]{4,3,2,1,0:T(8,128)(2,1)} %reshape.151), kind=kLoop, calls=%fused_computation.60 | loop fusion | bytes 12582912 | tf_op jit(solution)/shard_map/slice | solution.py:23
  201.3 7.1 %copy.39 = bf16[64,16,1,16,64]{0,4,3,1,2:T(8,128)(2,1)} copy(bf16[64,16,1,16,64]{4,3,2,1,0:T(8,128)(2,1)} %get-tuple-element.7) | data formatting | bytes 4194304
  208.4 8.4 %fusion.6 = f32[16,16,64,64]{2,3,1,0:T(8,128)S(1)} fusion(bf16[64,16,1,16,64]{4,3,2,1,0:T(8,128)(2,1)} %get-tuple-element.8, bf16[64,16,1,16,64]{4,3,2,1,0:T(8,128)(2,1)} %get-tuple-element.9), kind=kOutput, calls=%fused_computation.16 | convolution fusion | flops 134217728 | bytes 8388608 | tf_op jit(solution)/shard_map/lghe,mghe->ghlm/dot_general | solution.py:27
  216.8 5.8 %fusion.43 = (f32[16,16,64]{2,1,0:T(8,128)S(1)}, f32[16,16,64,64]{2,3,1,0:T(8,128)}) fusion(f32[16,16,64,64]{2,3,1,0:T(8,128)S(1)} %fusion.6, pred[16,64]{1,0:T(8,128)(4,1)S(1)} %iota_compare_fusion), kind=kOutput, calls=%fused_computation.63 | output fusion | flops 6291519 | bytes 8455168 | tf_op jit(solution)/shard_map/sub | solution.py:31
  222.7 6.8 %fusion.24 = bf16[16,16,64,64]{3,2,1,0:T(8,128)(2,1)} fusion(f32[16,16,64,64]{2,3,1,0:T(8,128)} %get-tuple-element.16, f32[16,16,64]{2,1,0:T(8,128)S(1)} %get-tuple-element.15, bf16[64,16,1,16,64]{0,4,3,1,2:T(8,128)(2,1)S(1)} %copy-done.3), kind=kOutput, calls=%fused_computation.43 | convolution fusion | flops 137363456 | bytes 8454144 | tf_op jit(solution)/shard_map/ghlm,mghe->lghe/dot_general | solution.py:34
  229.4 5.6 %copy.31 = bf16[64,16,1024]{2,1,0:T(8,128)(2,1)} copy(bf16[64,16,1024]{0,2,1:T(8,128)(2,1)} %bitcast.85) | data formatting | bytes 4194304 | tf_op jit(solution)/shard_map/dot_general | solution.py:39
  235.1 4.5 %fusion.10 = bf16[64,16,1024]{2,1,0:T(8,128)(2,1)S(1)} fusion(bf16[64,16,1024]{2,1,0:T(8,128)(2,1)} %copy.31, bf16[1024,1024]{1,0:T(8,128)(2,1)} %param.13, bf16[16,4,16,1024]{3,2,0,1:T(8,128)(2,1)S(1)} %all-to-all-done.1), kind=kOutput, calls=%fused_computation.25 | convolution fusion | flops 2150629376 | bytes 8388608 | tf_op jit(solution)/shard_map/dot_general | solution.py:39
  239.6 0.0 copy-start.1
  239.6 28.1 %all_to_all.29 = bf16[4,16,16,1024]{3,2,1,0:T(8,128)(2,1)S(1)} all-to-all(bf16[4,16,16,1024]{3,2,1,0:T(8,128)(2,1)S(1)} %bitcast.86), channel_id=1, replica_groups=mesh['seq'=64,'grp'=4] {'grp'}, dimensions={0} | all-to-all | bytes 4194304 | tf_op jit(solution)/shard_map/all_to_all | solution.py:69
  267.7 1.5 copy.32
  (12 shorter events, 0.1 us)
Async XLA Ops:
  0.0 2.9 %copy-start = (bf16[1024,1024]{1,0:T(8,128)(2,1)S(1)}, bf16[1024,1024]{1,0:T(8,128)(2,1)}, u32[]{:S(2)}) copy-start(bf16[1024,1024]{1,0:T(8,128)(2,1)} %param.8) | copy-start | bytes 6291460
  2.9 13.7 %copy-start.7 = (s32[1,64]{1,0:T(1,128)S(1)}, s32[1,64]{1,0:T(1,128)}, u32[]{:S(2)}) copy-start(s32[1,64]{1,0:T(1,128)} %param.10) | copy-start | bytes 772
  4.9 62.7 %copy-start.5 = (f32[1024]{0:T(1024)S(1)}, f32[1024]{0:T(1024)}, u32[]{:S(2)}) copy-start(f32[1024]{0:T(1024)} %param.14) | copy-start | bytes 12292
  4.9 62.1 %all-to-all-start = ((bf16[64,16,1024]{2,1,0:T(8,128)(2,1)}), bf16[64,16,1024]{2,1,0:T(8,128)(2,1)S(1)}, u32[]{:S(2)}, u32[]{:S(2)}) async-start(bf16[64,16,1024]{2,1,0:T(8,128)(2,1)} %gather_fusion), calls=%async_computation | async-start | bytes 4194304 | tf_op jit(solution)/shard_map/all_to_all | solution.py:51
  117.5 4.5 %copy-start.2 = (bf16[16,64,1,16,64]{1,4,3,0,2:T(8,128)(2,1)S(1)}, bf16[16,64,1,16,64]{1,4,3,0,2:T(8,128)(2,1)}, u32[]{:S(2)}) copy-start(bf16[16,64,1,16,64]{1,4,3,0,2:T(8,128)(2,1)} %copy.36) | copy-start | bytes 6291460
  122.0 4.9 %copy-start.4 = (bf16[1024,1024]{1,0:T(8,128)(2,1)S(1)}, bf16[1024,1024]{1,0:T(8,128)(2,1)}, u32[]{:S(2)}) copy-start(bf16[1024,1024]{1,0:T(8,128)(2,1)} %param.13) | copy-start | bytes 6291460
  131.0 6.2 %copy-start.8 = (s32[1,64]{1,0:T(1,128)S(1)}, s32[1,64]{1,0:T(1,128)}, u32[]{:S(2)}) copy-start(s32[1,64]{1,0:T(1,128)} %param.11) | copy-start | bytes 772
  132.7 31.5 %copy-start.6 = (f32[1024]{0:T(1024)S(1)}, f32[1024]{0:T(1024)}, u32[]{:S(2)}) copy-start(f32[1024]{0:T(1024)} %param.15) | copy-start | bytes 12292
  132.7 31.0 %all-to-all-start.1 = ((bf16[16,4,16,1024]{3,2,0,1:T(8,128)(2,1)}), bf16[16,4,16,1024]{3,2,0,1:T(8,128)(2,1)S(1)}, u32[]{:S(2)}, u32[]{:S(2)}) async-start(bf16[16,4,16,1024]{3,2,0,1:T(8,128)(2,1)} %copy.26), calls=%async_computation.1 | async-start | bytes 4194304 | tf_op jit(solution)/shard_map/all_to_all | solution.py:61
  216.8 5.8 %copy-start.3 = (bf16[64,16,1,16,64]{0,4,3,1,2:T(8,128)(2,1)S(1)}, bf16[64,16,1,16,64]{0,4,3,1,2:T(8,128)(2,1)}, u32[]{:S(2)}) copy-start(bf16[64,16,1,16,64]{0,4,3,1,2:T(8,128)(2,1)} %copy.39) | copy-start | bytes 6291460
  239.6 29.6 %copy-start.1 = (bf16[1024,1024]{1,0:T(8,128)(2,1)S(1)}, bf16[1024,1024]{1,0:T(8,128)(2,1)}, u32[]{:S(2)}) copy-start(bf16[1024,1024]{1,0:T(8,128)(2,1)} %param.8) | copy-start | bytes 6291460
where the time goes:
time: 271 us; the launch traced here: 269 us
  waiting for transfers between devices  76.5 us (28%)
  local copies, waits for them, and re-layouts  75.6 us (28%)
  matrix products  55.5 us (20%)
  blocking collectives  28.1 us (10%)
  other arithmetic  17 us (6%)
  starting transfers between devices  16.3 us (6%)
    all_to_all x1, waiting for transfers between devices, on_device(): lax.all_to_all(outgoing, 'seq', split_axis=0, concat_axis=0, tiled=True)  50.3 us
    reshape x2, local copies, waits for them, and re-layouts, project(): proj = proj.reshape(first_dim, second_dim, 3, HEADS, width // HEADS)  31.9 us
    all_to_all x1, blocking collectives, on_device(): lax.all_to_all(second.reshape(n_grp, local_times, share, width), 'grp', s...  28.1 us
    all_to_all x1, waiting for transfers between devices, on_device(): lax.all_to_all(spread, 'grp', split_axis=1, concat_axis=0, tiled=True)  26.2 us
    dot_general x2, matrix products, project(): jnp.dot(normed.reshape(first_dim * second_dim, width), w_qkv, preferred_e...  22.7 us
    slice x2, local copies, waits for them, and re-layouts, project(): return (proj[:, :, 0], proj[:, :, 1], proj[:, :, 2])  18.4 us
    unnamed x20, local copies, waits for them, and re-layouts  14.3 us
    dot_general x2, matrix products, attend(): jnp.einsum(form_scores, query, keys, preferred_element_type=jnp.float32)  14.2 us
  transfers between devices with their start and end apart: 2, of which 2 were waited for; matrix products, arithmetic and copies ran while one was open for 0% of the time, Pallas kernels for 0%

commit v1 on v0

v1 whole, which is shorter than its diff:
```python
import functools
import math

import jax
import jax.numpy as jnp
from jax import lax
from jax.experimental import pallas as pl
from jax.experimental.pallas import tpu as pltpu
from jax.sharding import PartitionSpec as P

MESH = pl.DeviceIdType.MESH
BF16 = jnp.bfloat16
F32 = jnp.float32

WIDTH = 1024
ROW = 16
TILE = 256
COLS = 512
SCALE = 64**-0.5 * math.log2(math.e)


def hop(e):
    return jnp.where(e % 2 == 1, (e + 1) // 2, lax.rem(8 - e // 2, 8))


def one_hot(source_row):
    rows = lax.broadcasted_iota(jnp.int32, (TILE, TILE), 0)
    cols = lax.broadcasted_iota(jnp.int32, (TILE, TILE), 1)
    return jnp.where(rows == source_row(cols), 1.0, 0.0).astype(BF16)


def kernel(
    order_ref,
    patches_hbm,
    info_ref,
    wqkv_hbm,
    wout_hbm,
    gain_var_ref,
    gain_time_ref,
    out_hbm,
    patches,
    wqkv,
    wout,
    info,
    perms,
    outgoing,
    packed,
    spread,
    turned,
    back,
    landed,
    resid,
    normed,
    qkv,
    qkv_time,
    context,
    result,
    load_sem,
    info_sem,
    send1,
    recv1,
    send2,
    recv2,
    send3,
    recv3,
    out_sem,
):
    seq = lax.axis_index("seq")
    y = lax.axis_index("grp")
    z, x, c = seq // 8, lax.rem(seq // 2, 4), lax.rem(seq, 2)
    chip = z * 4 + x
    to_core = x // 2
    member = y * 2 + c

    loads = [
        pltpu.make_async_copy(patches_hbm, patches, load_sem.at[0]),
        pltpu.make_async_copy(wqkv_hbm, wqkv, load_sem.at[1]),
        pltpu.make_async_copy(wout_hbm, wout, load_sem.at[2]),
    ]
    for load in loads:
        load.start()

    barrier = pltpu.get_barrier_semaphore()

    @pl.loop(0, 32)
    def _(j):
        source = ((j // 4) * 4 + 2 * c + lax.rem(j // 2, 2)) * 2 + lax.rem(j, 2)

        @pl.when(source != seq)
        def _():
            pl.semaphore_signal(
                barrier, inc=1, device_id={"seq": source, "grp": y}, device_id_type=MESH
            )

    @pl.loop(1, 8)
    def _(j):
        pl.semaphore_signal(
            barrier,
            inc=1,
            device_id={
                "seq": chip * 2 + lax.rem(c + j, 2),
                "grp": lax.rem(y + j // 2, 4),
            },
            device_id_type=MESH,
        )

    perms[0] = one_hot(lambda r: (r % 64) * 4 + r // 64)
    perms[1] = one_hot(lambda r: ((r // 4) % 8) * 32 + (r // 32) * 4 + r % 4)

    def to_time(r):
        e = ((r // 32) % 2) * 4 + r % 4
        k = 2 * lax.rem(z - hop(e) + 8, 8) + (r // 4) % 2
        return ((r // 8) % 4) * 64 + k * 4 + r // 64

    perms[2] = one_hot(to_time)
    perms[3] = one_hot(lambda r: ((r // 4) % 4) * 64 + (r // 16) * 4 + r % 4)

    pl.semaphore_wait(barrier, 39 - jnp.where(to_core == c, 1, 0))
    loads[0].wait()

    info_local = pltpu.make_async_copy(info_ref, info.at[c], info_sem.at[0])
    info_remote = pltpu.make_async_remote_copy(
        src_ref=info_ref,
        dst_ref=info.at[c],
        send_sem=info_sem.at[1],
        recv_sem=info_sem.at[2],
        device_id={"seq": chip * 2 + 1 - c, "grp": y},
        device_id_type=MESH,
    )

    def place1(jj):
        e, dx, p = lax.rem(jj // 4, 8), lax.rem(jj, 4), jj // 32
        to_chip = lax.rem(z + hop(e), 8) * 4 + lax.rem(x + dx, 4)
        slot = p * 32 + e * 4 + lax.rem(x, 2) * 2 + c
        return to_chip, to_chip * 2 + to_core, p, slot

    def rows1(ref, slot):
        return ref.at[pl.ds(pl.multiple_of(slot * ROW, ROW), ROW)]

    def send_blocks(begin, end):
        @pl.loop(begin, end)
        def _(jj):
            to_chip, dest, p, slot = place1(jj)
            block = order_ref[to_chip * 2 + p]
            outgoing[jj] = patches[block]

            @pl.when(dest != seq)
            def _():
                pltpu.make_async_remote_copy(
                    src_ref=outgoing.at[jj],
                    dst_ref=rows1(packed, slot),
                    send_sem=send1.at[jj],
                    recv_sem=recv1.at[slot],
                    device_id={"seq": dest, "grp": y},
                    device_id_type=MESH,
                ).start()

            @pl.when(dest == seq)
            def _():
                pltpu.make_async_copy(
                    outgoing.at[jj], rows1(packed, slot), recv1.at[slot]
                ).start()

    send_blocks(0, 64)
    info_local.start()
    info_remote.start()

    lanes = lax.broadcasted_iota(jnp.int32, (64, 128), 1)
    first_half = lanes < 64
    diag_rows = lax.broadcasted_iota(jnp.int32, (128, 128), 0) // 64
    diag_cols = lax.broadcasted_iota(jnp.int32, (128, 128), 1) // 64
    ones = jnp.where(diag_rows == diag_cols, 1.0, 0.0).astype(BF16)
    pos = lax.broadcasted_iota(jnp.int32, (64, 128), 1) % 64
    key_time = (
        16 * ((pos // 8) % 4)
        + 2 * lax.rem(z - hop((pos // 32) * 4 + pos % 4) + 8, 8)
        + (pos // 4) % 2
    ).astype(F32)

    def norm(rows, gain_ref):
        wide = rows.astype(F32)
        mean = jnp.sum(wide * wide, axis=-1, keepdims=True) * (1.0 / WIDTH)
        normed[...] = (wide * lax.rsqrt(mean + 1e-05) * gain_ref[...]).astype(BF16)

    def attend(source, row, target, target_row, keep):
        zero = jnp.zeros((64, 128), BF16)
        rows = pl.ds(pl.multiple_of(row, 64), 64)
        for pair in range(8):
            query = source[rows, pair * 128 : pair * 128 + 128]
            keys = source[rows, WIDTH + pair * 128 : WIDTH + pair * 128 + 128]
            values = source[rows, 2 * WIDTH + pair * 128 : 2 * WIDTH + pair * 128 + 128]
            keys = jnp.concatenate(
                [jnp.where(first_half, keys, zero), jnp.where(first_half, zero, keys)], 0
            )
            values = jnp.concatenate(
                [jnp.where(first_half, values, zero), jnp.where(first_half, zero, values)], 0
            )
            scores = lax.dot_general(
                query, keys, (((1,), (1,)), ((), ())), preferred_element_type=F32
            )
            scores = jnp.where(keep, scores, -1e30)
            low = jnp.max(jnp.where(first_half, scores, -jnp.inf), axis=-1, keepdims=True)
            high = jnp.max(jnp.where(first_half, -jnp.inf, scores), axis=-1, keepdims=True)
            expo = jnp.exp2((scores - jnp.where(first_half, low, high)) * SCALE).astype(BF16)
            both = jnp.dot(
                expo, jnp.concatenate([values, ones], 1), preferred_element_type=F32
            )
            target[pl.ds(pl.multiple_of(target_row, 64), 64), pair * 128 : pair * 128 + 128] = (
                both[:, :128] / both[:, 128:]
            ).astype(BF16)

    def variates(p, q):
        at = p * 512 + q * TILE

        @pl.loop(0, 16)
        def _(j):
            slot = p * 32 + q * 16 + j
            pltpu.make_async_copy(
                rows1(packed, slot), rows1(packed, slot), recv1.at[slot]
            ).wait()

        norm(packed[at : at + TILE, :], gain_var_ref)

        @pl.loop(0, 3 * WIDTH // COLS)
        def _(n):
            cols = pl.ds(pl.multiple_of(n * COLS, COLS), COLS)
            qkv[:, cols] = jnp.dot(
                normed[...], wqkv[:, cols], preferred_element_type=F32
            ).astype(BF16)

        keep = info[p, :64, :] > 0.5

        @pl.loop(0, 4)
        def _(u):
            attend(qkv, u * 64, context, u * 64, keep)

        @pl.loop(0, WIDTH // COLS)
        def _(n):
            cols = pl.ds(pl.multiple_of(n * COLS, COLS), COLS)
            first = (
                jnp.dot(context[...], wout[:, cols], preferred_element_type=F32)
                + packed[at : at + TILE, cols].astype(F32)
            ).astype(BF16)
            spread[2 * p + q, :, cols] = jnp.dot(
                perms[0], first, preferred_element_type=F32
            ).astype(BF16)

        for j in range(8):
            dest_y, dest_c = lax.rem(y + j // 2, 4), lax.rem(c + j, 2)
            dest = dest_y * 2 + dest_c
            source = spread.at[2 * p + q, pl.ds(pl.multiple_of(dest * 32, 32), 32)]
            target = turned.at[2 * p + q, pl.ds(pl.multiple_of(member * 32, 32), 32)]
            if j == 0:
                pltpu.make_async_copy(source, target, recv2.at[2 * p + q, member]).start()
            else:
                pltpu.make_async_remote_copy(
                    src_ref=source,
                    dst_ref=target,
                    send_sem=send2.at[2 * p + q, j],
                    recv_sem=recv2.at[2 * p + q, member],
                    device_id={"seq": chip * 2 + dest_c, "grp": dest_y},
                    device_id_type=MESH,
                ).start()

    def project_time(p, q):
        @pl.loop(0, 8)
        def _(j):
            part = turned.at[2 * p + q, pl.ds(pl.multiple_of(j * 32, 32), 32)]
            pltpu.make_async_copy(part, part, recv2.at[2 * p + q, j]).wait()

        rows = jnp.dot(perms[1], turned[2 * p + q], preferred_element_type=F32).astype(BF16)
        for v in range(8):
            resid[v * 64 + q * 32 : v * 64 + q * 32 + 32, :] = rows[v * 32 : v * 32 + 32, :]
        norm(rows, gain_time_ref)

        @pl.loop(0, 3 * WIDTH // COLS)
        def _(n):
            cols = pl.ds(pl.multiple_of(n * COLS, COLS), COLS)
            proj = jnp.dot(normed[...], wqkv[:, cols], preferred_element_type=F32).astype(BF16)
            for v in range(8):
                qkv_time[v * 64 + q * 32 : v * 64 + q * 32 + 32, cols] = proj[
                    v * 32 : v * 32 + 32, :
                ]

    def times(p, h):
        @pl.loop(0, 4)
        def _(u):
            length = info[p, pl.ds(64 + member * 8 + h * 4 + u, 1), :]
            keep = key_time < jnp.broadcast_to(length, (64, 128))
            attend(qkv_time, h * TILE + u * 64, context, u * 64, keep)

        @pl.loop(0, WIDTH // COLS)
        def _(n):
            cols = pl.ds(pl.multiple_of(n * COLS, COLS), COLS)
            second = (
                jnp.dot(context[...], wout[:, cols], preferred_element_type=F32)
                + resid[h * TILE : h * TILE + TILE, cols].astype(F32)
            ).astype(BF16)
            second = jnp.dot(perms[2], second, preferred_element_type=F32).astype(BF16)
            back[2 * p + h, :, :, :, cols] = second.reshape(4, 4, ROW, COLS)

        for j in range(4):
            dest_y = lax.rem(y + j, 4)
            source = back.at[2 * p + h, dest_y]
            target = landed.at[:, member * 2 + h]

            def send():
                pltpu.make_async_remote_copy(
                    src_ref=source,
                    dst_ref=target,
                    send_sem=send3.at[2 * p + h, j],
                    recv_sem=recv3.at[member * 2 + h],
                    device_id={"seq": chip * 2 + p, "grp": dest_y},
                    device_id_type=MESH,
                ).start()

            if j == 0:
                pl.when(c != p)(send)

                @pl.when(c == p)
                def _():
                    pltpu.make_async_copy(source, target, recv3.at[member * 2 + h]).start()
            else:
                send()

    loads[1].wait()
    loads[2].wait()
    info_local.wait()
    info_remote.wait()

    variates(0, 0)
    variates(0, 1)
    project_time(0, 0)
    project_time(0, 1)
    times(0, 0)
    times(0, 1)
    variates(1, 0)
    variates(1, 1)
    project_time(1, 0)
    project_time(1, 1)
    times(1, 0)
    times(1, 1)

    @pl.loop(0, 16)
    def _(j):
        part = landed.at[:, j]
        pltpu.make_async_copy(part, part, recv3.at[j]).wait()

    writes = []
    for h in range(4):
        result[h * TILE : h * TILE + TILE, :] = jnp.dot(
            perms[3], landed[h].reshape(TILE, WIDTH), preferred_element_type=F32
        ).astype(BF16)
        rows = pl.ds(h * TILE, TILE)
        write = pltpu.make_async_copy(result.at[rows], out_hbm.at[rows], out_sem.at[h])
        write.start()
        writes.append(write)

    @pl.loop(0, 64)
    def _(jj):
        _, dest, _, _ = place1(jj)

        @pl.when(dest != seq)
        def _():
            pltpu.make_async_copy(outgoing.at[jj], outgoing.at[jj], send1.at[jj]).wait()

    for pq in range(4):
        for j in range(1, 8):
            part = spread.at[pq, pl.ds(0, 32)]
            pltpu.make_async_copy(part, part, send2.at[pq, j]).wait()
        for j in range(4):

            def drain():
                part = back.at[pq, j]
                pltpu.make_async_copy(part, part, send3.at[pq, j]).wait()

            if j == 0:
                pl.when(c != pq // 2)(drain)
            else:
                drain()

    for write in writes:
        write.wait()


def on_device(patches, dest_map, series_ids, lengths, w_qkv, w_out, gain_var, gain_time):
    index = jnp.arange(64, dtype=jnp.int32)
    order = jnp.sum(
        jnp.where(dest_map[0][None, :] == index[:, None], index[None, :], 0), axis=1
    ).astype(jnp.int32)
    ids = series_ids[0]
    same = (ids[:, None] == jnp.concatenate([ids, ids])[None, :]).astype(F32)
    valid = jnp.broadcast_to(lengths[0].astype(F32)[:, None], (64, 128))
    info = jnp.concatenate([same, valid], axis=0)
    any_space = pl.BlockSpec(memory_space=pl.ANY)
    vmem = pl.BlockSpec(memory_space=pltpu.VMEM)
    return pl.pallas_call(
        kernel,
        out_shape=jax.ShapeDtypeStruct((1024, WIDTH), BF16),
        in_specs=[
            pl.BlockSpec(memory_space=pltpu.SMEM),
            any_space,
            vmem,
            any_space,
            any_space,
            vmem,
            vmem,
        ],
        out_specs=any_space,
        scratch_shapes=[
            pltpu.VMEM((64, ROW, WIDTH), BF16),
            pltpu.VMEM((WIDTH, 3 * WIDTH), BF16),
            pltpu.VMEM((WIDTH, WIDTH), BF16),
            pltpu.VMEM((2, 128, 128), F32),
            pltpu.VMEM((4, TILE, TILE), BF16),
            pltpu.VMEM((64, ROW, WIDTH), BF16),
            pltpu.VMEM((1024, WIDTH), BF16),
            pltpu.VMEM((4, TILE, WIDTH), BF16),
            pltpu.VMEM((4, TILE, WIDTH), BF16),
            pltpu.VMEM((4, 4, 4, ROW, WIDTH), BF16),
            pltpu.VMEM((4, 16, ROW, WIDTH), BF16),
            pltpu.VMEM((512, WIDTH), BF16),
            pltpu.VMEM((TILE, WIDTH), BF16),
            pltpu.VMEM((TILE, 3 * WIDTH), BF16),
            pltpu.VMEM((512, 3 * WIDTH), BF16),
            pltpu.VMEM((TILE, WIDTH), BF16),
            pltpu.VMEM((1024, WIDTH), BF16),
            pltpu.SemaphoreType.DMA((3,)),
            pltpu.SemaphoreType.DMA((3,)),
            pltpu.SemaphoreType.DMA((64,)),
            pltpu.SemaphoreType.DMA((64,)),
            pltpu.SemaphoreType.DMA((4, 8)),
            pltpu.SemaphoreType.DMA((4, 8)),
            pltpu.SemaphoreType.DMA((4, 4)),
            pltpu.SemaphoreType.DMA((16,)),
            pltpu.SemaphoreType.DMA((4,)),
        ],
        compiler_params=pltpu.CompilerParams(
            collective_id=0, has_side_effects=True, vmem_limit_bytes=52 << 20
        ),
        cost_estimate=pl.CostEstimate(
            flops=20_000_000_000, bytes_accessed=12_000_000, transcendentals=4_000_000
        ),
        name="pack_layer",
    )(
        order,
        patches.reshape(64, ROW, WIDTH),
        info,
        w_qkv,
        w_out,
        gain_var.reshape(1, WIDTH),
        gain_time.reshape(1, WIDTH),
    )


def solution(mesh):
    return jax.shard_map(
        on_device,
        mesh=mesh,
        in_specs=(
            P(("seq", "grp"), None),
            P(("seq", "grp"), None),
            P("seq", None),
            P("seq", None),
            P(),
            P(),
            P(),
            P(),
        ),
        out_specs=P(("seq", "grp"), None),
        check_vma=False,
    )
```

time: 271 us -> 156 us (0.58)
  the two profiles are of different devices: /device:TPU:32 before, /device:TPU:1 now
where the time goes in v1:
time: 156 us
  Pallas kernels  148 us (95%)
  local copies, waits for them, and re-layouts  4.53 us (3%)
  other arithmetic  3.04 us (2%)
    pallas_call x1, Pallas kernels, on_device(): pl.pallas_call(kernel, out_shape=jax.ShapeDtypeStruct((1024, WIDTH), BF16...  148 us
    unnamed x5, local copies, waits for them, and re-layouts  4.45 us

profile of v1, /device:TPU:1, one launch (start us, length us, event | category | flops | bytes accessed | tf_op | source)
XLA Modules:
  0.0 155.9 jit_solution(14009468570118618006)
XLA Ops:
  0.0 0.8 select_reduce_fusion.order_ref
  0.8 0.8 pad_add_fusion
  1.6 0.7 convert_bitcast_fusion
  2.2 0.1 pad.1.clone
  2.3 0.7 compare_convert_fusion
  3.0 0.1 pad_maximum_fusion.info_ref
  3.1 0.0 copy-start
  3.1 0.7 copy-done
  3.8 0.0 copy-start.1
  3.8 0.7 copy-done.1
  4.5 148.3 %pack_layer.1 = bf16[1024,1024]{1,0:T(8,128)(2,1)} custom-call(s32[64]{0:T(128)S(1)} %select_reduce_fusion.order_ref, bf16[64,16,1024]{2,1,0:T(8,128)(2,1)} %bitcast.11, f32[128,128]{1,0:T(8,128)S(1)} %pad_maximum_fusion.info_ref, bf16[1024,3072]{1,0:T(8,128)(2,1)} %wqkv_hbm.1, bf16[1024,1024]{1,0:T(8,128)(2,1)} %wout_hbm.1, f32[1,1024]{1,0:T(1,128)S(1)} %bitcast.7, ...), custom_call_target="tpu_custom_call" | custom-call | flops 20000000000 | bytes 12000000 | tf_op jit(solution)/shard_map/pack_layer/pallas_call | solution.py:397
  152.9 3.1 %copy.10 = bf16[1024,1024]{1,0:T(8,128)(2,1)} copy(bf16[1024,1024]{1,0:T(8,128)(2,1)} %pack_layer.1) | data formatting | bytes 4194304
Async XLA Ops:
  3.1 0.7 copy-start
  3.8 0.7 copy-start.1

commit v2 on v1

v2 whole, which is shorter than its diff:
```python
import functools
import math

import jax
import jax.numpy as jnp
from jax import lax
from jax.experimental import pallas as pl
from jax.experimental.pallas import tpu as pltpu
from jax.sharding import PartitionSpec as P

MESH = pl.DeviceIdType.MESH
BF16 = jnp.bfloat16
F32 = jnp.float32

WIDTH = 1024
ROW = 16
TILE = 256
COLS = 512
SCALE = 64**-0.5 * math.log2(math.e)


def hop(e):
    return jnp.where(e % 2 == 1, (e + 1) // 2, lax.rem(8 - e // 2, 8))


def one_hot(source_row):
    rows = lax.broadcasted_iota(jnp.int32, (TILE, TILE), 0)
    cols = lax.broadcasted_iota(jnp.int32, (TILE, TILE), 1)
    return jnp.where(rows == source_row(cols), 1.0, 0.0).astype(BF16)


def kernel(
    order_ref,
    patches_hbm,
    ids_hbm,
    lengths_hbm,
    wqkv_hbm,
    wout_hbm,
    gain_var_hbm,
    gain_time_hbm,
    landed,
    patches,
    small,
    gains,
    info_own,
    wqkv,
    wout,
    info,
    perms,
    outgoing,
    packed,
    spread,
    turned,
    back,
    resid,
    normed,
    qkv,
    qkv_time,
    context,
    load_sem,
    info_sem,
    send1,
    recv1,
    send2,
    recv2,
    send3,
    recv3,
):
    seq = lax.axis_index("seq")
    y = lax.axis_index("grp")
    z, x, c = seq // 8, lax.rem(seq // 2, 4), lax.rem(seq, 2)
    chip = z * 4 + x
    to_core = x // 2
    member = y * 2 + c

    loads = [
        pltpu.make_async_copy(patches_hbm, patches, load_sem.at[0]),
        pltpu.make_async_copy(ids_hbm, small.at[pl.ds(0, 1)], load_sem.at[1]),
        pltpu.make_async_copy(lengths_hbm, small.at[pl.ds(1, 1)], load_sem.at[2]),
        pltpu.make_async_copy(gain_var_hbm, gains.at[0], load_sem.at[3]),
        pltpu.make_async_copy(gain_time_hbm, gains.at[1], load_sem.at[4]),
        pltpu.make_async_copy(wqkv_hbm, wqkv, load_sem.at[5]),
        pltpu.make_async_copy(wout_hbm, wout, load_sem.at[6]),
    ]
    for load in loads:
        load.start()

    barrier = pltpu.get_barrier_semaphore()

    @pl.loop(0, 32)
    def _(j):
        source = ((j // 4) * 4 + 2 * c + lax.rem(j // 2, 2)) * 2 + lax.rem(j, 2)

        @pl.when(source != seq)
        def _():
            pl.semaphore_signal(
                barrier, inc=1, device_id={"seq": source, "grp": y}, device_id_type=MESH
            )

    @pl.loop(1, 8)
    def _(j):
        pl.semaphore_signal(
            barrier,
            inc=1,
            device_id={
                "seq": chip * 2 + lax.rem(c + j, 2),
                "grp": lax.rem(y + j // 2, 4),
            },
            device_id_type=MESH,
        )

    perms[0] = one_hot(lambda r: (r % 64) * 4 + r // 64)
    perms[1] = one_hot(lambda r: ((r // 4) % 8) * 32 + (r // 32) * 4 + r % 4)

    def to_time(r):
        e = ((r // 32) % 2) * 4 + r % 4
        k = 2 * lax.rem(z - hop(e) + 8, 8) + (r // 4) % 2
        return ((r // 8) % 4) * 64 + k * 4 + r // 64

    perms[2] = one_hot(to_time)

    pl.semaphore_wait(barrier, 39 - jnp.where(to_core == c, 1, 0))
    loads[0].wait()

    def place1(jj):
        e, dx, p = lax.rem(jj // 4, 8), lax.rem(jj, 4), jj // 32
        to_chip = lax.rem(z + hop(e), 8) * 4 + lax.rem(x + dx, 4)
        slot = p * 32 + e * 4 + lax.rem(x, 2) * 2 + c
        return to_chip, to_chip * 2 + to_core, p, slot

    def send_blocks(begin, end):
        @pl.loop(begin, end)
        def _(jj):
            to_chip, dest, p, slot = place1(jj)
            block = order_ref[to_chip * 2 + p]
            outgoing[jj] = patches[block]

            @pl.when(dest != seq)
            def _():
                pltpu.make_async_remote_copy(
                    src_ref=outgoing.at[jj],
                    dst_ref=packed.at[slot],
                    send_sem=send1.at[jj],
                    recv_sem=recv1.at[slot],
                    device_id={"seq": dest, "grp": y},
                    device_id_type=MESH,
                ).start()

            @pl.when(dest == seq)
            def _():
                pltpu.make_async_copy(
                    outgoing.at[jj], packed.at[slot], recv1.at[slot]
                ).start()

    send_blocks(0, 64)

    loads[1].wait()
    loads[2].wait()
    eye = lax.broadcasted_iota(jnp.int32, (64, 64), 0) == lax.broadcasted_iota(
        jnp.int32, (64, 64), 1
    )
    ids = small[0:1, :].astype(F32)
    ids_down = jnp.sum(jnp.where(eye, ids, 0.0), axis=1, keepdims=True)
    info_own[:64, :64] = jnp.where(ids_down == ids, 1.0, 0.0)
    info_own[:64, 64:] = jnp.where(ids_down == ids, 1.0, 0.0)
    count_down = jnp.sum(
        jnp.where(eye, small[1:2, :].astype(F32), 0.0), axis=1, keepdims=True
    )
    info_own[64:, :] = jnp.broadcast_to(count_down, (64, 128))
    info_local = pltpu.make_async_copy(info_own, info.at[c], info_sem.at[0])
    info_remote = pltpu.make_async_remote_copy(
        src_ref=info_own,
        dst_ref=info.at[c],
        send_sem=info_sem.at[1],
        recv_sem=info_sem.at[2],
        device_id={"seq": chip * 2 + 1 - c, "grp": y},
        device_id_type=MESH,
    )
    info_local.start()
    info_remote.start()

    lanes = lax.broadcasted_iota(jnp.int32, (64, 128), 1)
    first_half = lanes < 64
    diag_rows = lax.broadcasted_iota(jnp.int32, (128, 128), 0) // 64
    diag_cols = lax.broadcasted_iota(jnp.int32, (128, 128), 1) // 64
    ones = jnp.where(diag_rows == diag_cols, 1.0, 0.0).astype(BF16)
    pos = lax.broadcasted_iota(jnp.int32, (64, 128), 1) % 64
    key_time = (
        16 * ((pos // 8) % 4)
        + 2 * lax.rem(z - hop((pos // 32) * 4 + pos % 4) + 8, 8)
        + (pos // 4) % 2
    ).astype(F32)

    def norm(rows, gain):
        wide = rows.astype(F32)
        mean = jnp.sum(wide * wide, axis=-1, keepdims=True) * (1.0 / WIDTH)
        normed[...] = (wide * lax.rsqrt(mean + 1e-05) * gains[gain]).astype(BF16)

    zero = jnp.zeros((64, 128), BF16)

    def apart(pair):
        return jnp.concatenate(
            [jnp.where(first_half, pair, zero), jnp.where(first_half, zero, pair)], 0
        )

    def attend(source, begin, keeps):
        parts = [(u, pair * 128) for u in range(4) for pair in range(8)]
        expos = []
        scored = []
        for u, col in parts:
            rows = slice(begin + u * 64, begin + u * 64 + 64)
            scores = lax.dot_general(
                source[rows, col : col + 128],
                apart(source[rows, WIDTH + col : WIDTH + col + 128]),
                (((1,), (1,)), ((), ())),
                preferred_element_type=F32,
            )
            scored.append(jnp.where(keeps[u], scores, -1e30))
        for scores in scored:
            low = jnp.max(jnp.where(first_half, scores, -jnp.inf), axis=-1, keepdims=True)
            high = jnp.max(jnp.where(first_half, -jnp.inf, scores), axis=-1, keepdims=True)
            expos.append(
                jnp.exp2((scores - jnp.where(first_half, low, high)) * SCALE).astype(BF16)
            )
        for (u, col), expo in zip(parts, expos):
            rows = slice(begin + u * 64, begin + u * 64 + 64)
            values = apart(source[rows, 2 * WIDTH + col : 2 * WIDTH + col + 128])
            both = jnp.dot(
                expo, jnp.concatenate([values, ones], 1), preferred_element_type=F32
            )
            context[u * 64 : u * 64 + 64, col : col + 128] = (
                both[:, :128] / both[:, 128:]
            ).astype(BF16)

    def variates(p, q):
        @pl.loop(0, 16)
        def _(j):
            slot = p * 32 + q * 16 + j
            pltpu.make_async_copy(packed.at[slot], packed.at[slot], recv1.at[slot]).wait()

        blocks = pl.ds(pl.multiple_of(p * 32 + q * 16, 16), 16)
        norm(packed[blocks].reshape(TILE, WIDTH), 0)
        for col in range(0, 3 * WIDTH, COLS):
            cols = slice(col, col + COLS)
            qkv[:, cols] = jnp.dot(
                normed[...], wqkv[:, cols], preferred_element_type=F32
            ).astype(BF16)
        keep = info[p, :64, :] > 0.5
        attend(qkv, 0, [keep] * 4)
        for col in range(0, WIDTH, COLS):
            cols = slice(col, col + COLS)
            normed[:, cols] = (
                jnp.dot(context[...], wout[:, cols], preferred_element_type=F32)
                + packed[blocks, :, cols].reshape(TILE, COLS).astype(F32)
            ).astype(BF16)
        for col in range(0, WIDTH, COLS):
            cols = slice(col, col + COLS)
            spread[2 * p + q, :, cols] = jnp.dot(
                perms[0], normed[:, cols], preferred_element_type=F32
            ).astype(BF16)

        for j in range(8):
            dest_y, dest_c = lax.rem(y + j // 2, 4), lax.rem(c + j, 2)
            dest = dest_y * 2 + dest_c
            source = spread.at[2 * p + q, pl.ds(pl.multiple_of(dest * 32, 32), 32)]
            target = turned.at[2 * p + q, pl.ds(pl.multiple_of(member * 32, 32), 32)]
            if j == 0:
                pltpu.make_async_copy(source, target, recv2.at[2 * p + q, member]).start()
            else:
                pltpu.make_async_remote_copy(
                    src_ref=source,
                    dst_ref=target,
                    send_sem=send2.at[2 * p + q, j],
                    recv_sem=recv2.at[2 * p + q, member],
                    device_id={"seq": chip * 2 + dest_c, "grp": dest_y},
                    device_id_type=MESH,
                ).start()

    def project_time(p, q):
        @pl.loop(0, 8)
        def _(j):
            part = turned.at[2 * p + q, pl.ds(pl.multiple_of(j * 32, 32), 32)]
            pltpu.make_async_copy(part, part, recv2.at[2 * p + q, j]).wait()

        rows = jnp.dot(perms[1], turned[2 * p + q], preferred_element_type=F32).astype(BF16)
        for v in range(8):
            resid[v * 64 + q * 32 : v * 64 + q * 32 + 32, :] = rows[v * 32 : v * 32 + 32, :]
        norm(rows, 1)

        for col in range(0, 3 * WIDTH, COLS):
            cols = slice(col, col + COLS)
            proj = jnp.dot(normed[...], wqkv[:, cols], preferred_element_type=F32).astype(BF16)
            for v in range(8):
                qkv_time[v * 64 + q * 32 : v * 64 + q * 32 + 32, cols] = proj[
                    v * 32 : v * 32 + 32, :
                ]

    def times(p, h):
        keeps = []
        for u in range(4):
            length = info[p, pl.ds(64 + member * 8 + h * 4 + u, 1), :]
            keeps.append(key_time < jnp.broadcast_to(length, (64, 128)))
        attend(qkv_time, h * TILE, keeps)
        for col in range(0, WIDTH, COLS):
            cols = slice(col, col + COLS)
            normed[:, cols] = (
                jnp.dot(context[...], wout[:, cols], preferred_element_type=F32)
                + resid[h * TILE : h * TILE + TILE, cols].astype(F32)
            ).astype(BF16)
        for col in range(0, WIDTH, COLS):
            cols = slice(col, col + COLS)
            second = jnp.dot(perms[2], normed[:, cols], preferred_element_type=F32).astype(BF16)
            back[2 * p + h, :, :, :, cols] = second.reshape(4, 4, ROW, COLS)

        for j in range(4):
            dest_y = lax.rem(y + j, 4)
            source = back.at[2 * p + h, dest_y]
            target = landed.at[:, member * 2 + h]

            def send():
                pltpu.make_async_remote_copy(
                    src_ref=source,
                    dst_ref=target,
                    send_sem=send3.at[2 * p + h, j],
                    recv_sem=recv3.at[member * 2 + h],
                    device_id={"seq": chip * 2 + p, "grp": dest_y},
                    device_id_type=MESH,
                ).start()

            if j == 0:
                pl.when(c != p)(send)

                @pl.when(c == p)
                def _():
                    pltpu.make_async_copy(source, target, recv3.at[member * 2 + h]).start()
            else:
                send()

    for load in loads[3:]:
        load.wait()
    info_local.wait()
    info_remote.wait()

    @pl.loop(0, 2)
    def _(p):
        variates(p, 0)
        variates(p, 1)
        project_time(p, 0)
        project_time(p, 1)
        times(p, 0)
        times(p, 1)

    @pl.loop(0, 16)
    def _(j):
        part = landed.at[:, j]
        pltpu.make_async_copy(part, part, recv3.at[j]).wait()

    @pl.loop(0, 64)
    def _(jj):
        _, dest, _, _ = place1(jj)

        @pl.when(dest != seq)
        def _():
            pltpu.make_async_copy(outgoing.at[jj], outgoing.at[jj], send1.at[jj]).wait()

    for pq in range(4):
        for j in range(1, 8):
            part = spread.at[pq, pl.ds(0, 32)]
            pltpu.make_async_copy(part, part, send2.at[pq, j]).wait()
        for j in range(4):

            def drain():
                part = back.at[pq, j]
                pltpu.make_async_copy(part, part, send3.at[pq, j]).wait()

            if j == 0:
                pl.when(c != pq // 2)(drain)
            else:
                drain()


def in_time_order(landed_ref, out_hbm, result, sems):
    perm = one_hot(lambda r: ((r // 4) % 4) * 64 + (r // 16) * 4 + r % 4)
    writes = []
    for h in range(4):
        rows = pl.ds(h * TILE, TILE)
        result[rows, :] = jnp.dot(
            perm, landed_ref[h].reshape(TILE, WIDTH), preferred_element_type=F32
        ).astype(BF16)
        writes.append(pltpu.make_async_copy(result.at[rows], out_hbm.at[rows], sems.at[h]))
        writes[-1].start()
    for write in writes:
        write.wait()


def on_device(patches, dest_map, series_ids, lengths, w_qkv, w_out, gain_var, gain_time):
    index = jnp.arange(64, dtype=jnp.int32)
    order = jnp.sum(
        jnp.where(dest_map[0][None, :] == index[:, None], index[None, :], 0), axis=1
    ).astype(jnp.int32)
    any_space = pl.BlockSpec(memory_space=pl.ANY)
    landed = pl.pallas_call(
        kernel,
        out_shape=pltpu.VMEM((4, 16, ROW, WIDTH), BF16),
        in_specs=[pl.BlockSpec(memory_space=pltpu.SMEM)] + [any_space] * 7,
        out_specs=pl.BlockSpec(memory_space=pltpu.VMEM),
        scratch_shapes=[
            pltpu.VMEM((64, ROW, WIDTH), BF16),
            pltpu.VMEM((8, 64), jnp.int32),
            pltpu.VMEM((2, 1, WIDTH), F32),
            pltpu.VMEM((128, 128), F32),
            pltpu.VMEM((WIDTH, 3 * WIDTH), BF16),
            pltpu.VMEM((WIDTH, WIDTH), BF16),
            pltpu.VMEM((2, 128, 128), F32),
            pltpu.VMEM((3, TILE, TILE), BF16),
            pltpu.VMEM((64, ROW, WIDTH), BF16),
            pltpu.VMEM((64, ROW, WIDTH), BF16),
            pltpu.VMEM((4, TILE, WIDTH), BF16),
            pltpu.VMEM((4, TILE, WIDTH), BF16),
            pltpu.VMEM((4, 4, 4, ROW, WIDTH), BF16),
            pltpu.VMEM((512, WIDTH), BF16),
            pltpu.VMEM((TILE, WIDTH), BF16),
            pltpu.VMEM((TILE, 3 * WIDTH), BF16),
            pltpu.VMEM((512, 3 * WIDTH), BF16),
            pltpu.VMEM((TILE, WIDTH), BF16),
            pltpu.SemaphoreType.DMA((7,)),
            pltpu.SemaphoreType.DMA((3,)),
            pltpu.SemaphoreType.DMA((64,)),
            pltpu.SemaphoreType.DMA((64,)),
            pltpu.SemaphoreType.DMA((4, 8)),
            pltpu.SemaphoreType.DMA((4, 8)),
            pltpu.SemaphoreType.DMA((4, 4)),
            pltpu.SemaphoreType.DMA((16,)),
        ],
        compiler_params=pltpu.CompilerParams(
            collective_id=0, has_side_effects=True, vmem_limit_bytes=52 << 20
        ),
        cost_estimate=pl.CostEstimate(
            flops=20_000_000_000, bytes_accessed=12_000_000, transcendentals=4_000_000
        ),
        name="pack_layer",
    )(
        order,
        patches.reshape(64, ROW, WIDTH),
        series_ids,
        lengths,
        w_qkv,
        w_out,
        gain_var.reshape(1, WIDTH),
        gain_time.reshape(1, WIDTH),
    )
    return pl.pallas_call(
        in_time_order,
        out_shape=jax.ShapeDtypeStruct((1024, WIDTH), BF16),
        in_specs=[pl.BlockSpec(memory_space=pltpu.VMEM)],
        out_specs=any_space,
        scratch_shapes=[pltpu.VMEM((1024, WIDTH), BF16), pltpu.SemaphoreType.DMA((4,))],
        compiler_params=pltpu.CompilerParams(vmem_limit_bytes=8 << 20),
        name="time_order",
    )(landed)


def solution(mesh):
    return jax.shard_map(
        on_device,
        mesh=mesh,
        in_specs=(
            P(("seq", "grp"), None),
            P(("seq", "grp"), None),
            P("seq", None),
            P("seq", None),
            P(),
            P(),
            P(),
            P(),
        ),
        out_specs=P(("seq", "grp"), None),
        check_vma=False,
    )
```

time: 156 us -> 103 us (0.66)
  Pallas kernels: 148 us -> 101 us
  local copies, waits for them, and re-layouts: 4.53 us -> 0 us
  other arithmetic: 3.04 us -> 1.28 us
    pallas_call x1 -> x2, Pallas kernels: 148 us -> 101 us  [the longest x1 99.1 us: on_device(): pl.pallas_call(kernel, out_shape=pltpu.VMEM((4, 16, ROW, WIDTH), BF16), i...]
    unnamed x5 -> x0, local copies, waits for them, and re-layouts: 4.45 us -> none
where the time goes in v2:
time: 103 us; the launch traced here: 102 us
  Pallas kernels  101 us (98%)
  other arithmetic  1.28 us (1%)
    pallas_call x1, Pallas kernels, on_device(): pl.pallas_call(kernel, out_shape=pltpu.VMEM((4, 16, ROW, WIDTH), BF16), i...  99.1 us

profile of v2, /device:TPU:1, one launch (start us, length us, event | category | flops | bytes accessed | tf_op | source)
XLA Modules:
  0.0 102.1 jit_solution(4243644912402862703)
XLA Ops:
  0.0 1.3 %select_reduce_fusion.order_ref = s32[64]{0:T(128)} fusion(s32[64]{0:T(128)} %bitcast.7), kind=kLoop, calls=%fused_computation | loop fusion | flops 12224 | bytes 512 | tf_op jit(solution)/shard_map/reduce_sum | solution.py:398
  1.3 99.1 %pack_layer.1.landed_ref = bf16[4,16,16,1024]{3,2,1,0:T(8,128)(2,1)S(1)} custom-call(s32[64]{0:T(128)} %select_reduce_fusion.order_ref, bf16[64,16,1024]{2,1,0:T(8,128)(2,1)} %bitcast.4, s32[1,64]{1,0:T(1,128)} %ids_hbm.1, s32[1,64]{1,0:T(1,128)} %lengths_hbm.1, bf16[1024,3072]{1,0:T(8,128)(2,1)} %wqkv_hbm.1, bf16[1024,1024]{1,0:T(8,128)(2,1)} %wout_hbm.1, ...), custom_call_target="tpu_custom_call" | custom-call | flops 20000000000 | bytes 12000000 | tf_op jit(solution)/shard_map/pack_layer/pallas_call | solution.py:402
  100.4 1.7 %time_order.1 = bf16[1024,1024]{1,0:T(8,128)(2,1)} custom-call(bf16[4,16,16,1024]{3,2,1,0:T(8,128)(2,1)S(1)} %pack_layer.1.landed_ref), custom_call_target="tpu_custom_call" | custom-call | tf_op jit(solution)/shard_map/time_order/pallas_call | solution.py:452

commit v3 on v2

--- a/solution.py
+++ b/solution.py
@@ -19,19 +19,27 @@
 SCALE = 64**-0.5 * math.log2(math.e)
 
 
+PARTNERS = ((0, 0), (1, 0), (3, 1), (1, 1), (3, 0), (2, 0), (2, 1), (0, 1))
+CHUNKS = ((0, 4), (4, 2), (6, 2))
+
+
 def hop(e):
+    return jnp.where((e & 1) == 1, (e + 1) >> 1, (8 - (e >> 1)) & 7)
+
+
+def hop_scalar(e):
     return jnp.where(e % 2 == 1, (e + 1) // 2, lax.rem(8 - e // 2, 8))
 
 
-def one_hot(source_row):
-    rows = lax.broadcasted_iota(jnp.int32, (TILE, TILE), 0)
-    cols = lax.broadcasted_iota(jnp.int32, (TILE, TILE), 1)
-    return jnp.where(rows == source_row(cols), 1.0, 0.0).astype(BF16)
+def one_hot(size, target):
+    rows = lax.broadcasted_iota(jnp.int32, (size, size), 0)
+    cols = lax.broadcasted_iota(jnp.int32, (1, size), 1)
+    return jnp.where(rows == target(cols), 1.0, 0.0).astype(BF16)
 
 
 def kernel(
-    order_ref,
     patches_hbm,
+    dest_hbm,
     ids_hbm,
     lengths_hbm,
     wqkv_hbm,
@@ -43,10 +51,13 @@
     small,
     gains,
     info_own,
+    order_down,
+    order_ref,
     wqkv,
     wout,
     info,
     perms,
+    perms_half,
     outgoing,
     packed,
     spread,
@@ -75,14 +86,15 @@
 
     loads = [
         pltpu.make_async_copy(patches_hbm, patches, load_sem.at[0]),
-        pltpu.make_async_copy(ids_hbm, small.at[pl.ds(0, 1)], load_sem.at[1]),
-        pltpu.make_async_copy(lengths_hbm, small.at[pl.ds(1, 1)], load_sem.at[2]),
-        pltpu.make_async_copy(gain_var_hbm, gains.at[0], load_sem.at[3]),
-        pltpu.make_async_copy(gain_time_hbm, gains.at[1], load_sem.at[4]),
-        pltpu.make_async_copy(wqkv_hbm, wqkv, load_sem.at[5]),
-        pltpu.make_async_copy(wout_hbm, wout, load_sem.at[6]),
+        pltpu.make_async_copy(dest_hbm, small.at[pl.ds(2, 1)], load_sem.at[1]),
+        pltpu.make_async_copy(ids_hbm, small.at[pl.ds(0, 1)], load_sem.at[2]),
+        pltpu.make_async_copy(lengths_hbm, small.at[pl.ds(1, 1)], load_sem.at[3]),
+        pltpu.make_async_copy(gain_var_hbm, gains.at[0], load_sem.at[4]),
+        pltpu.make_async_copy(gain_time_hbm, gains.at[1], load_sem.at[5]),
+        pltpu.make_async_copy(wqkv_hbm, wqkv, load_sem.at[6]),
+        pltpu.make_async_copy(wout_hbm, wout, load_sem.at[7]),
     ]
-    for load in loads:
+    for load in loads[:4]:
         load.start()
 
     barrier = pltpu.get_barrier_semaphore()
@@ -109,22 +121,32 @@
             device_id_type=MESH,
         )
 
-    perms[0] = one_hot(lambda r: (r % 64) * 4 + r // 64)
-    perms[1] = one_hot(lambda r: ((r // 4) % 8) * 32 + (r // 32) * 4 + r % 4)
-
-    def to_time(r):
-        e = ((r // 32) % 2) * 4 + r % 4
-        k = 2 * lax.rem(z - hop(e) + 8, 8) + (r // 4) % 2
-        return ((r // 8) % 4) * 64 + k * 4 + r // 64
-
-    perms[2] = one_hot(to_time)
+    eye = lax.broadcasted_iota(jnp.int32, (64, 64), 0) == lax.broadcasted_iota(
+        jnp.int32, (64, 64), 1
+    )
+
+    def down(row):
+        return jnp.sum(jnp.where(eye, row.astype(F32), 0.0), axis=1, keepdims=True)
+
+    loads[1].wait()
+    pack = lax.broadcasted_iota(jnp.int32, (64, 64), 1).astype(F32)
+    number = lax.broadcasted_iota(jnp.int32, (64, 64), 0)
+    order = jnp.sum(
+        jnp.where(down(small[2:3, :]) == pack, number, 0), axis=0, keepdims=True
+    )
+    order_down[...] = jnp.minimum(order, 63)
+    to_scalars = pltpu.make_async_copy(order_down, order_ref, load_sem.at[8])
+    to_scalars.start()
 
     pl.semaphore_wait(barrier, 39 - jnp.where(to_core == c, 1, 0))
+    to_scalars.wait()
     loads[0].wait()
+    for load in loads[4:]:
+        load.start()
 
     def place1(jj):
         e, dx, p = lax.rem(jj // 4, 8), lax.rem(jj, 4), jj // 32
-        to_chip = lax.rem(z + hop(e), 8) * 4 + lax.rem(x + dx, 4)
+        to_chip = lax.rem(z + hop_scalar(e), 8) * 4 + lax.rem(x + dx, 4)
         slot = p * 32 + e * 4 + lax.rem(x, 2) * 2 + c
         return to_chip, to_chip * 2 + to_core, p, slot
 
@@ -132,7 +154,7 @@
         @pl.loop(begin, end)
         def _(jj):
             to_chip, dest, p, slot = place1(jj)
-            block = order_ref[to_chip * 2 + p]
+            block = jnp.minimum(order_ref[0, to_chip * 2 + p], 63)
             outgoing[jj] = patches[block]
 
             @pl.when(dest != seq)
@@ -154,19 +176,13 @@
 
     send_blocks(0, 64)
 
-    loads[1].wait()
     loads[2].wait()
-    eye = lax.broadcasted_iota(jnp.int32, (64, 64), 0) == lax.broadcasted_iota(
-        jnp.int32, (64, 64), 1
-    )
+    loads[3].wait()
     ids = small[0:1, :].astype(F32)
-    ids_down = jnp.sum(jnp.where(eye, ids, 0.0), axis=1, keepdims=True)
-    info_own[:64, :64] = jnp.where(ids_down == ids, 1.0, 0.0)
-    info_own[:64, 64:] = jnp.where(ids_down == ids, 1.0, 0.0)
-    count_down = jnp.sum(
-        jnp.where(eye, small[1:2, :].astype(F32), 0.0), axis=1, keepdims=True
-    )
-    info_own[64:, :] = jnp.broadcast_to(count_down, (64, 128))
+    same = jnp.where(down(small[0:1, :]) == ids, 1.0, 0.0)
+    info_own[:64, :64] = same
+    info_own[:64, 64:] = same
+    info_own[64:, :] = jnp.broadcast_to(down(small[1:2, :]), (64, 128))
     info_local = pltpu.make_async_copy(info_own, info.at[c], info_sem.at[0])
     info_remote = pltpu.make_async_remote_copy(
         src_ref=info_own,
@@ -179,22 +195,45 @@
     info_local.start()
     info_remote.start()
 
+    def by_variate(times):
+        return lambda r: (r & 63) * times + (r >> 6)
+
+    def gathered(shift):
+        return lambda r: (
+            (((r >> shift) & 7) << (3 + shift))
+            + ((r >> (3 + shift)) << shift)
+            + (r & ((1 << shift) - 1))
+        )
+
+    def sent(pos):
+        early = pos < 32
+        e = jnp.where(early, pos & 3, 4 + ((pos >> 4) & 1) * 2 + (pos & 1))
+        sender = jnp.where(early, pos >> 2, (pos & 15) >> 1)
+        return sender, 2 * ((z - hop(e) + 8) & 7) + (sender & 1)
+
+    def to_time(r):
+        sender, k = sent(r & 63)
+        return (sender >> 1) * 64 + k * 4 + (r >> 6)
+
+    perms[0] = one_hot(TILE, by_variate(4))
+    perms[1] = one_hot(TILE, gathered(2))
+    perms[2] = one_hot(TILE, to_time)
+    perms_half[0] = one_hot(TILE // 2, by_variate(2))
+    perms_half[1] = one_hot(TILE // 2, gathered(1))
+
     lanes = lax.broadcasted_iota(jnp.int32, (64, 128), 1)
     first_half = lanes < 64
     diag_rows = lax.broadcasted_iota(jnp.int32, (128, 128), 0) // 64
     diag_cols = lax.broadcasted_iota(jnp.int32, (128, 128), 1) // 64
     ones = jnp.where(diag_rows == diag_cols, 1.0, 0.0).astype(BF16)
-    pos = lax.broadcasted_iota(jnp.int32, (64, 128), 1) % 64
-    key_time = (
-        16 * ((pos // 8) % 4)
-        + 2 * lax.rem(z - hop((pos // 32) * 4 + pos % 4) + 8, 8)
-        + (pos // 4) % 2
-    ).astype(F32)
+    key_sender, key_k = sent(lanes & 63)
+    key_time = (16 * (key_sender >> 1) + key_k).astype(F32)
 
     def norm(rows, gain):
+        size = rows.shape[0]
         wide = rows.astype(F32)
         mean = jnp.sum(wide * wide, axis=-1, keepdims=True) * (1.0 / WIDTH)
-        normed[...] = (wide * lax.rsqrt(mean + 1e-05) * gains[gain]).astype(BF16)
+        normed[:size] = (wide * lax.rsqrt(mean + 1e-05) * gains[gain]).astype(BF16)
 
     zero = jnp.zeros((64, 128), BF16)
 
@@ -204,7 +243,7 @@
         )
 
     def attend(source, begin, keeps):
-        parts = [(u, pair * 128) for u in range(4) for pair in range(8)]
+        parts = [(u, pair * 128) for u in range(len(keeps)) for pair in range(8)]
         expos = []
         scored = []
         for u, col in parts:
@@ -233,86 +272,97 @@
             ).astype(BF16)
 
     def variates(p, q):
-        @pl.loop(0, 16)
+        begin, count = CHUNKS[q]
+        size = count * 64
+
+        @pl.loop(0, count * 4)
         def _(j):
-            slot = p * 32 + q * 16 + j
+            slot = p * 32 + begin * 4 + j
             pltpu.make_async_copy(packed.at[slot], packed.at[slot], recv1.at[slot]).wait()
 
-        blocks = pl.ds(pl.multiple_of(p * 32 + q * 16, 16), 16)
-        norm(packed[blocks].reshape(TILE, WIDTH), 0)
+        blocks = pl.ds(pl.multiple_of(p * 32 + begin * 4, 4), count * 4)
+        norm(packed[blocks].reshape(size, WIDTH), 0)
         for col in range(0, 3 * WIDTH, COLS):
             cols = slice(col, col + COLS)
-            qkv[:, cols] = jnp.dot(
-                normed[...], wqkv[:, cols], preferred_element_type=F32
+            qkv[:size, cols] = jnp.dot(
+                normed[:size], wqkv[:, cols], preferred_element_type=F32
             ).astype(BF16)
         keep = info[p, :64, :] > 0.5
-        attend(qkv, 0, [keep] * 4)
+        attend(qkv, 0, [keep] * count)
         for col in range(0, WIDTH, COLS):
             cols = slice(col, col + COLS)
-            normed[:, cols] = (
-                jnp.dot(context[...], wout[:, cols], preferred_element_type=F32)
-                + packed[blocks, :, cols].reshape(TILE, COLS).astype(F32)
+            normed[:size, cols] = (
+                jnp.dot(context[:size], wout[:, cols], preferred_element_type=F32)
+                + packed[blocks, :, cols].reshape(size, COLS).astype(F32)
             ).astype(BF16)
+        perm = perms[0] if count == 4 else perms_half[0]
         for col in range(0, WIDTH, COLS):
             cols = slice(col, col + COLS)
-            spread[2 * p + q, :, cols] = jnp.dot(
-                perms[0], normed[:, cols], preferred_element_type=F32
+            spread[p, begin * 64 : begin * 64 + size, cols] = jnp.dot(
+                perm, normed[:size, cols], preferred_element_type=F32
             ).astype(BF16)
-
-        for j in range(8):
-            dest_y, dest_c = lax.rem(y + j // 2, 4), lax.rem(c + j, 2)
+        part = count * 8
+        for j, (dy, dc) in enumerate(PARTNERS):
+            dest_y, dest_c = lax.rem(y + dy, 4), lax.rem(c + dc, 2)
             dest = dest_y * 2 + dest_c
-            source = spread.at[2 * p + q, pl.ds(pl.multiple_of(dest * 32, 32), 32)]
-            target = turned.at[2 * p + q, pl.ds(pl.multiple_of(member * 32, 32), 32)]
+            source = spread.at[p, pl.ds(pl.multiple_of(begin * 64 + dest * part, 16), part)]
+            target = turned.at[p, pl.ds(pl.multiple_of(begin * 64 + member * part, 16), part)]
             if j == 0:
-                pltpu.make_async_copy(source, target, recv2.at[2 * p + q, member]).start()
+                pltpu.make_async_copy(source, target, recv2.at[p, q, member]).start()
             else:
                 pltpu.make_async_remote_copy(
                     src_ref=source,
                     dst_ref=target,
-                    send_sem=send2.at[2 * p + q, j],
-                    recv_sem=recv2.at[2 * p + q, member],
+                    send_sem=send2.at[p, q, j],
+                    recv_sem=recv2.at[p, q, member],
                     device_id={"seq": chip * 2 + dest_c, "grp": dest_y},
                     device_id_type=MESH,
                 ).start()
 
     def project_time(p, q):
+        begin, count = CHUNKS[q]
+        size, part = count * 64, count * 8
+
         @pl.loop(0, 8)
         def _(j):
-            part = turned.at[2 * p + q, pl.ds(pl.multiple_of(j * 32, 32), 32)]
-            pltpu.make_async_copy(part, part, recv2.at[2 * p + q, j]).wait()
-
-        rows = jnp.dot(perms[1], turned[2 * p + q], preferred_element_type=F32).astype(BF16)
+            piece = turned.at[p, pl.ds(pl.multiple_of(begin * 64 + j * part, 16), part)]
+            pltpu.make_async_copy(piece, piece, recv2.at[p, q, j]).wait()
+
+        perm = perms[1] if count == 4 else perms_half[1]
+        rows = jnp.dot(
+            perm, turned[p, begin * 64 : begin * 64 + size], preferred_element_type=F32
+        ).astype(BF16)
         for v in range(8):
-            resid[v * 64 + q * 32 : v * 64 + q * 32 + 32, :] = rows[v * 32 : v * 32 + 32, :]
+            at = v * 64 + begin * 8
+            resid[p, at : at + part, :] = rows[v * part : v * part + part, :]
         norm(rows, 1)
-
         for col in range(0, 3 * WIDTH, COLS):
             cols = slice(col, col + COLS)
-            proj = jnp.dot(normed[...], wqkv[:, cols], preferred_element_type=F32).astype(BF16)
+            proj = jnp.dot(
+                normed[:size], wqkv[:, cols], preferred_element_type=F32
+            ).astype(BF16)
             for v in range(8):
-                qkv_time[v * 64 + q * 32 : v * 64 + q * 32 + 32, cols] = proj[
-                    v * 32 : v * 32 + 32, :
-                ]
+                at = v * 64 + begin * 8
+                qkv_time[p, at : at + part, cols] = proj[v * part : v * part + part, :]
 
     def times(p, h):
         keeps = []
         for u in range(4):
             length = info[p, pl.ds(64 + member * 8 + h * 4 + u, 1), :]
             keeps.append(key_time < jnp.broadcast_to(length, (64, 128)))
-        attend(qkv_time, h * TILE, keeps)
+        attend(qkv_time.at[p], h * TILE, keeps)
         for col in range(0, WIDTH, COLS):
             cols = slice(col, col + COLS)
             normed[:, cols] = (
                 jnp.dot(context[...], wout[:, cols], preferred_element_type=F32)
-                + resid[h * TILE : h * TILE + TILE, cols].astype(F32)
+                + resid[p, h * TILE : h * TILE + TILE, cols].astype(F32)
             ).astype(BF16)
         for col in range(0, WIDTH, COLS):
             cols = slice(col, col + COLS)
             second = jnp.dot(perms[2], normed[:, cols], preferred_element_type=F32).astype(BF16)
             back[2 * p + h, :, :, :, cols] = second.reshape(4, 4, ROW, COLS)
 
-        for j in range(4):
+        for j in (1, 3, 2, 0):
             dest_y = lax.rem(y + j, 4)
             source = back.at[2 * p + h, dest_y]
             target = landed.at[:, member * 2 + h]
@@ -336,19 +386,27 @@
             else:
                 send()
 
-    for load in loads[3:]:
+    for load in loads[4:]:
         load.wait()
     info_local.wait()
     info_remote.wait()
 
-    @pl.loop(0, 2)
-    def _(p):
-        variates(p, 0)
-        variates(p, 1)
-        project_time(p, 0)
-        project_time(p, 1)
-        times(p, 0)
-        times(p, 1)
+    variates(0, 0)
+    project_time(0, 0)
+    variates(0, 1)
+    variates(0, 2)
+    project_time(0, 1)
+    project_time(0, 2)
+    times(0, 0)
+    variates(1, 0)
+    variates(1, 1)
+    variates(1, 2)
+    times(0, 1)
+    project_time(1, 0)
+    project_time(1, 1)
+    project_time(1, 2)
+    times(1, 0)
+    times(1, 1)
 
     @pl.loop(0, 16)
     def _(j):
@@ -363,10 +421,12 @@
         def _():
             pltpu.make_async_copy(outgoing.at[jj], outgoing.at[jj], send1.at[jj]).wait()
 
+    for p in range(2):
+        for q, (_, count) in enumerate(CHUNKS):
+            for j in range(1, 8):
+                part = spread.at[p, pl.ds(0, count * 8)]
+                pltpu.make_async_copy(part, part, send2.at[p, q, j]).wait()
     for pq in range(4):
-        for j in range(1, 8):
-            part = spread.at[pq, pl.ds(0, 32)]
-            pltpu.make_async_copy(part, part, send2.at[pq, j]).wait()
         for j in range(4):
 
             def drain():
@@ -380,7 +440,7 @@
 
 
 def in_time_order(landed_ref, out_hbm, result, sems):
-    perm = one_hot(lambda r: ((r // 4) % 4) * 64 + (r // 16) * 4 + r % 4)
+    perm = one_hot(TILE, lambda r: ((r >> 2) & 3) * 64 + (r >> 4) * 4 + (r & 3))
     writes = []
     for h in range(4):
         rows = pl.ds(h * TILE, TILE)
@@ -394,41 +454,40 @@
 
 
 def on_device(patches, dest_map, series_ids, lengths, w_qkv, w_out, gain_var, gain_time):
-    index = jnp.arange(64, dtype=jnp.int32)
-    order = jnp.sum(
-        jnp.where(dest_map[0][None, :] == index[:, None], index[None, :], 0), axis=1
-    ).astype(jnp.int32)
     any_space = pl.BlockSpec(memory_space=pl.ANY)
     landed = pl.pallas_call(
         kernel,
         out_shape=pltpu.VMEM((4, 16, ROW, WIDTH), BF16),
-        in_specs=[pl.BlockSpec(memory_space=pltpu.SMEM)] + [any_space] * 7,
+        in_specs=[any_space] * 8,
         out_specs=pl.BlockSpec(memory_space=pltpu.VMEM),
         scratch_shapes=[
             pltpu.VMEM((64, ROW, WIDTH), BF16),
             pltpu.VMEM((8, 64), jnp.int32),
             pltpu.VMEM((2, 1, WIDTH), F32),
             pltpu.VMEM((128, 128), F32),
+            pltpu.VMEM((1, 64), jnp.int32),
+            pltpu.SMEM((1, 64), jnp.int32),
             pltpu.VMEM((WIDTH, 3 * WIDTH), BF16),
             pltpu.VMEM((WIDTH, WIDTH), BF16),
             pltpu.VMEM((2, 128, 128), F32),
             pltpu.VMEM((3, TILE, TILE), BF16),
+            pltpu.VMEM((2, TILE // 2, TILE // 2), BF16),
             pltpu.VMEM((64, ROW, WIDTH), BF16),
             pltpu.VMEM((64, ROW, WIDTH), BF16),
-            pltpu.VMEM((4, TILE, WIDTH), BF16),
-            pltpu.VMEM((4, TILE, WIDTH), BF16),
+            pltpu.VMEM((2, 512, WIDTH), BF16),
+            pltpu.VMEM((2, 512, WIDTH), BF16),
             pltpu.VMEM((4, 4, 4, ROW, WIDTH), BF16),
-            pltpu.VMEM((512, WIDTH), BF16),
+            pltpu.VMEM((2, 512, WIDTH), BF16),
             pltpu.VMEM((TILE, WIDTH), BF16),
             pltpu.VMEM((TILE, 3 * WIDTH), BF16),
-            pltpu.VMEM((512, 3 * WIDTH), BF16),
+            pltpu.VMEM((2, 512, 3 * WIDTH), BF16),
             pltpu.VMEM((TILE, WIDTH), BF16),
-            pltpu.SemaphoreType.DMA((7,)),
+            pltpu.SemaphoreType.DMA((9,)),
             pltpu.SemaphoreType.DMA((3,)),
             pltpu.SemaphoreType.DMA((64,)),
             pltpu.SemaphoreType.DMA((64,)),
-            pltpu.SemaphoreType.DMA((4, 8)),
-            pltpu.SemaphoreType.DMA((4, 8)),
+            pltpu.SemaphoreType.DMA((2, 3, 8)),
+            pltpu.SemaphoreType.DMA((2, 3, 8)),
             pltpu.SemaphoreType.DMA((4, 4)),
             pltpu.SemaphoreType.DMA((16,)),
         ],
@@ -440,8 +499,8 @@
         ),
         name="pack_layer",
     )(
-        order,
         patches.reshape(64, ROW, WIDTH),
+        dest_map,
         series_ids,
         lengths,
         w_qkv,

time: 103 us -> 94.7 us (0.919)
  Pallas kernels: 101 us -> 94.4 us
  other arithmetic: 1.28 us -> 0 us
    pallas_call x1, Pallas kernels: 99.1 us -> 92.7 us  [on_device(): pl.pallas_call(kernel, out_shape=pltpu.VMEM((4, 16, ROW, WIDTH), BF16), i...]
    reduce_sum x1 -> x0, other arithmetic: 1.28 us -> none  [on_device(): jnp.sum(jnp.where(dest_map[0][None, :] == index[:, None], index[None, :],...]
where the time goes in v3:
time: 94.7 us; the launch traced here: 94.6 us
  Pallas kernels  94.4 us (100%)
    pallas_call x1, Pallas kernels, on_device(): pl.pallas_call(kernel, out_shape=pltpu.VMEM((4, 16, ROW, WIDTH), BF16), i...  92.7 us

profile of v3, /device:TPU:1, one launch (start us, length us, event | category | flops | bytes accessed | tf_op | source)
XLA Modules:
  0.0 94.6 jit_solution(17034288386188615522)
XLA Ops:
  0.0 92.7 %pack_layer.1.landed_ref = bf16[4,16,16,1024]{3,2,1,0:T(8,128)(2,1)S(1)} custom-call(bf16[64,16,1024]{2,1,0:T(8,128)(2,1)} %bitcast.3, s32[1,64]{1,0:T(1,128)} %dest_hbm.1, s32[1,64]{1,0:T(1,128)} %ids_hbm.1, s32[1,64]{1,0:T(1,128)} %lengths_hbm.1, bf16[1024,3072]{1,0:T(8,128)(2,1)} %wqkv_hbm.1, bf16[1024,1024]{1,0:T(8,128)(2,1)} %wout_hbm.1, ...), custom_call_target="tpu_custom_call" | custom-call | flops 20000000000 | bytes 12000000 | tf_op jit(solution)/shard_map/pack_layer/pallas_call | solution.py:458
  92.8 1.7 %time_order.1 = bf16[1024,1024]{1,0:T(8,128)(2,1)} custom-call(bf16[4,16,16,1024]{3,2,1,0:T(8,128)(2,1)S(1)} %pack_layer.1.landed_ref), custom_call_target="tpu_custom_call" | custom-call | tf_op jit(solution)/shard_map/time_order/pallas_call | solution.py:511

commit v4 on v3

--- a/solution.py
+++ b/solution.py
@@ -19,7 +19,7 @@
 SCALE = 64**-0.5 * math.log2(math.e)
 
 
-PARTNERS = ((0, 0), (1, 0), (3, 1), (1, 1), (3, 0), (2, 0), (2, 1), (0, 1))
+PARTNERS = ((0, 0), (2, 0), (2, 1), (1, 0), (3, 1), (1, 1), (3, 0), (0, 1))
 CHUNKS = ((0, 4), (4, 2), (6, 2))
 
 
@@ -362,7 +362,7 @@
             second = jnp.dot(perms[2], normed[:, cols], preferred_element_type=F32).astype(BF16)
             back[2 * p + h, :, :, :, cols] = second.reshape(4, 4, ROW, COLS)
 
-        for j in (1, 3, 2, 0):
+        for j in (2, 1, 3, 0):
             dest_y = lax.rem(y + j, 4)
             source = back.at[2 * p + h, dest_y]
             target = landed.at[:, member * 2 + h]

time: 94.7 us -> 93.3 us (0.985)
  Pallas kernels: 94.4 us -> 93 us
    pallas_call x1, Pallas kernels: 92.7 us -> 91.4 us  [on_device(): pl.pallas_call(kernel, out_shape=pltpu.VMEM((4, 16, ROW, WIDTH), BF16), i...]
where the time goes in v4:
time: 93.3 us; the launch traced here: 93.2 us
  Pallas kernels  93 us (100%)
    pallas_call x1, Pallas kernels, on_device(): pl.pallas_call(kernel, out_shape=pltpu.VMEM((4, 16, ROW, WIDTH), BF16), i...  91.4 us

profile of v4, /device:TPU:1, one launch (start us, length us, event | category | flops | bytes accessed | tf_op | source)
XLA Modules:
  0.0 93.2 jit_solution(16988008061205766707)
XLA Ops:
  0.0 91.4 %pack_layer.1.landed_ref = bf16[4,16,16,1024]{3,2,1,0:T(8,128)(2,1)S(1)} custom-call(bf16[64,16,1024]{2,1,0:T(8,128)(2,1)} %bitcast.3, s32[1,64]{1,0:T(1,128)} %dest_hbm.1, s32[1,64]{1,0:T(1,128)} %ids_hbm.1, s32[1,64]{1,0:T(1,128)} %lengths_hbm.1, bf16[1024,3072]{1,0:T(8,128)(2,1)} %wqkv_hbm.1, bf16[1024,1024]{1,0:T(8,128)(2,1)} %wout_hbm.1, ...), custom_call_target="tpu_custom_call" | custom-call | flops 20000000000 | bytes 12000000 | tf_op jit(solution)/shard_map/pack_layer/pallas_call | solution.py:458
  91.4 1.7 %time_order.1 = bf16[1024,1024]{1,0:T(8,128)(2,1)} custom-call(bf16[4,16,16,1024]{3,2,1,0:T(8,128)(2,1)S(1)} %pack_layer.1.landed_ref), custom_call_target="tpu_custom_call" | custom-call | tf_op jit(solution)/shard_map/time_order/pallas_call | solution.py:511
